TPU v7x, 512 devices: a whole 4x4x16 slice. The times are simulated.
512 devices in a mesh: gy: 16 (over y, x), gz: 32 (over z, core).
Axes of the slice: x: 4, y: 4, z: 16, core: 2. Of those that a mesh axis runs over, the one named last changes fastest.
Arguments:
- field: float32 [256, 128, 11, 512], P('gy', 'gz'), as said below
- start_x: float32 [512, 60], replicated, may hold values from -6 to 6
- start_y: float32 [256, 60], replicated, may hold values from -6 to 6
Outputs:
- factor_x: float32 [512, 60], replicated
- factor_y: float32 [256, 60], P('gy')
- core: float32 [60, 128, 660], P(None, 'gz')
Inputs may be any that keep to these rules, and one draw needn't show every extreme that they name: `field`: every entry is a real value; rows and columns carry varying scales.
All inputs are finite; a program needn't handle non-finite values.
Results may differ from a plain program's by a relative error of at most 0.0003.
Values sent between devices are 32-bit elements; how exact they have to be, the bound alone decides.
No kernel may reach another device: no remote copies, remote signals or barrier semaphores. Data moves between devices by JAX's collectives and lax.ppermute only.
A program may use at most 64 MiB of HBM per device.

v0:
```python
import jax
import jax.numpy as jnp
from jax import lax
from jax.sharding import PartitionSpec as P

ITERS = 4


def product(left, right):
    return jnp.dot(left, right, precision=lax.Precision.HIGHEST, preferred_element_type=jnp.float32)


def orthonormal(matrix):
    small = product(matrix.T, matrix)
    lower = jnp.linalg.cholesky(small)
    return lax.linalg.triangular_solve(lower, matrix, left_side=False, lower=True, transpose_a=True)


def per_device(field, start_x, start_y):
    rows_y, rows_z, count_var, width_x = field.shape
    rank = start_x.shape[1]
    flat = field.reshape(rows_y * rows_z * count_var, width_x)
    columns = flat.shape[0] * lax.axis_size("gy") * lax.axis_size("gz")
    factor_x = start_x
    gram_x = lax.psum(product(flat.T, flat), ("gy", "gz")) / columns
    for step in range(ITERS):
        factor_x = orthonormal(product(gram_x, factor_x))
    reduced = product(flat, factor_x).reshape(rows_y, rows_z * count_var * rank)
    columns_y = rows_z * count_var * rank * lax.axis_size("gz")
    total_y = rows_y * lax.axis_size("gy")
    first_row = lax.axis_index("gy") * rows_y
    whole = lax.all_gather(reduced, "gy", axis=0, tiled=True)
    gram_y = lax.psum(product(whole, whole.T), "gz") / columns_y
    factor_full = start_y
    for step in range(ITERS):
        factor_full = orthonormal(product(gram_y, factor_full))
    core = product(factor_full.T, whole)
    factor_y = lax.dynamic_slice_in_dim(factor_full, first_row, rows_y, 0)
    core = core / jnp.sqrt(jnp.float32(width_x * total_y))
    return (factor_x, factor_y, core.reshape(rank, rows_z, count_var * rank))


def solution(mesh):
    placed = (P("gy", "gz", None, None), P(), P())
    return jax.shard_map(
        per_device,
        mesh=mesh,
        in_specs=placed,
        out_specs=(P(), P("gy", None), P(None, "gz", None)),
        check_vma=False,
    )
```

profile of v0, /device:TPU:1, one launch (start us, length us, event | category | flops | bytes accessed | tf_op | source)
XLA Modules:
  0.0 878.7 jit_solution(5208822924482310710)
XLA Ops:
  7.2 6.2 fusion.2
  13.7 1.9 copy.23
  15.6 1.3 reshape.32
  16.9 469.0 %all-reduce.3.cloned.1.call-done = f32[512,512]{1,0:T(8,128)} async-done(((f32[512,512]{1,0:T(8,128)}), f32[512,512]{1,0:T(8,128)}) %all-reduce.3.cloned.1.call-update) | async-done | bytes 1048592 | tf_op jit(solution)/shard_map/psum | solution.py:25
  485.9 2.5 fusion.11
  488.4 0.3 fusion.67
  488.7 5.5 cholesky.134
  494.3 0.6 compare_reduce_fusion.7
  494.9 0.7 fusion.29
  495.6 4.6 custom-call.14
  500.1 0.3 convolution_bitcast_fusion.4
  500.5 1.2 fusion.9
  502.0 5.5 cholesky.145
  507.6 0.6 compare_reduce_fusion.6
  508.2 0.7 fusion.30
  508.9 4.6 custom-call.15
  513.5 0.3 convolution_bitcast_fusion.3
  513.8 1.2 fusion.7
  515.0 0.3 fusion.69
  515.3 5.5 cholesky.156
  520.9 0.6 compare_reduce_fusion.5
  521.5 0.7 fusion.31
  522.2 4.6 custom-call.16
  526.8 0.3 convolution_bitcast_fusion.2
  527.1 1.2 fusion.5
  528.3 0.3 fusion.70
  528.6 5.5 cholesky.167
  534.2 0.6 compare_reduce_fusion.4
  534.8 0.7 fusion.32
  535.5 4.6 custom-call.17
  540.1 0.3 convolution_bitcast_fusion.1
  540.4 1.4 convolution_bitcast_fusion
  542.0 0.8 reshape.33
  542.9 0.3 all-reduce.5.cloned.1.call-start
  543.2 58.9 %all-gather.2.cloned.1.call-done = f32[256,2640]{1,0:T(8,128)} async-done(((f32[16,2640]{1,0:T(8,128)}), f32[256,2640]{1,0:T(8,128)}) %all-gather.2.cloned.1.call-update) | async-done | bytes 2703376 | tf_op jit(solution)/shard_map/all_gather | solution.py:32
  602.1 5.8 fusion.71
  607.9 206.0 %all-reduce.5.cloned.1.call-done = f32[256,256]{1,0:T(8,128)} async-done(((f32[256,256]{1,0:T(8,128)}), f32[256,256]{1,0:T(8,128)}) %all-reduce.5.cloned.1.call-update) | async-done | bytes 262160 | tf_op jit(solution)/shard_map/psum | solution.py:33
  813.9 1.4 fusion.23
  815.6 5.5 cholesky.178
  821.1 0.6 compare_reduce_fusion.3
  821.7 0.7 fusion.33
  822.4 4.6 custom-call.18
  827.0 0.3 convolution_bitcast_fusion.8
  827.3 1.3 fusion.21
  828.9 5.5 cholesky.189
  834.4 0.6 compare_reduce_fusion.2
  835.1 0.7 fusion.34
  835.7 4.6 custom-call.19
  840.3 0.3 convolution_bitcast_fusion.7
  840.6 1.3 fusion.19
  842.3 5.5 cholesky.200
  847.8 0.6 compare_reduce_fusion.1
  848.4 0.7 fusion.35
  849.1 4.6 custom-call.20
  853.7 0.3 convolution_bitcast_fusion.6
  854.0 0.4 fusion.17
  854.6 5.5 cholesky.211
  860.2 0.6 compare_reduce_fusion
  860.8 0.7 fusion.36
  861.5 4.6 custom-call.21
  866.1 0.3 convolution_bitcast_fusion.5
  866.4 2.4 convolution_multiply_fusion
  868.8 2.6 reshape.34
  871.5 0.7 copy.29
  (50 shorter events, 2.7 us)
Async XLA Ops:
  7.2 478.7 %copy-start = (f32[512,60]{0,1:T(8,128)S(1)}, f32[512,60]{0,1:T(8,128)}, u32[]{:S(2)}) copy-start(f32[512,60]{0,1:T(8,128)} %param.9) | copy-start | bytes 368644
  7.2 478.7 %all-reduce.3.cloned.1.call-start = ((), (), s32[]{:S(2)}) async-start(), calls=%async_computation | async-start | bytes 2097152 | tf_op jit(solution)/shard_map/psum | solution.py:25
  13.5 588.6 %all-gather.2.cloned.1.call-start = ((), (), s32[]{:S(2)}) async-start(), calls=%async_computation.1 | async-start | bytes 2924544 | tf_op jit(solution)/shard_map/all_gather | solution.py:32
  485.9 14.6 %copy-start.2 = (f32[512,512]{1,0:T(8,128)S(1)}, f32[512,512]{1,0:T(8,128)}, u32[]{:S(2)}) copy-start(f32[512,512]{1,0:T(8,128)} %all-reduce.3.cloned.1.call-done) | copy-start | bytes 3145732
  513.8 26.6 %copy-start.3 = (f32[704,512]{1,0:T(8,128)S(1)}, f32[704,512]{1,0:T(8,128)}, u32[]{:S(2)}) copy-start(f32[704,512]{1,0:T(8,128)} %reshape.32) | copy-start | bytes 4325380
  540.4 67.4 %copy-start.5 = (f32[512,60]{0,1:T(8,128)}, f32[512,60]{0,1:T(8,128)S(1)}, u32[]{:S(2)}) copy-start(f32[512,60]{0,1:T(8,128)S(1)} %convolution_bitcast_fusion.1) | copy-start | bytes 368644
  542.9 271.0 %copy-start.6 = (f32[256,60]{0,1:T(8,128)S(1)}, f32[256,60]{0,1:T(8,128)}, u32[]{:S(2)}) copy-start(f32[256,60]{0,1:T(8,128)} %param.10) | copy-start | bytes 184324
  542.9 271.0 %all-reduce.5.cloned.1.call-start = ((), (), s32[]{:S(2)}) async-start(), calls=%async_computation.2 | async-start | bytes 524288 | tf_op jit(solution)/shard_map/psum | solution.py:33
  607.9 258.5 %copy-start.1 = (f32[256,2640]{1,0:T(8,128)S(1)}, f32[256,2640]{1,0:T(8,128)}, u32[]{:S(2)}) copy-start(f32[256,2640]{1,0:T(8,128)} %all-gather.2.cloned.1.call-done) | copy-start | bytes 8110084
  813.9 40.1 %copy-start.4 = (f32[256,256]{1,0:T(8,128)S(1)}, f32[256,256]{1,0:T(8,128)}, u32[]{:S(2)}) copy-start(f32[256,256]{1,0:T(8,128)} %all-reduce.5.cloned.1.call-done) | copy-start | bytes 786436
Sparse Core Ops, SparseCore 0:
  13.6 472.2 all-reduce.2
  543.0 59.0 all-gather.1
  608.0 205.8 all-reduce.4
where the time goes:
time: 879 us
  waiting for transfers between devices  734 us (84%)
  other arithmetic  91.3 us (10%)
  matrix products  30.5 us (3%)
  between operations  14.1 us (2%)
    psum x1, waiting for transfers between devices, per_device(): gram_x = lax.psum(product(flat.T, flat), ('gy', 'gz')) / columns  469 us
    psum x1, waiting for transfers between devices, per_device(): gram_y = lax.psum(product(whole, whole.T), 'gz') / columns_y  206 us
    all_gather x1, waiting for transfers between devices, per_device(): whole = lax.all_gather(reduced, 'gy', axis=0, tiled=True)  58.9 us
    another operation x24, other arithmetic, orthonormal(): lower = jnp.linalg.cholesky(small)  49.3 us
    another operation x16, other arithmetic, orthonormal(): lax.linalg.triangular_solve(lower, matrix, left_side=False, lower=True, t...  41.9 us
    dot_general x20, matrix products, product(): jnp.dot(left, right, precision=lax.Precision.HIGHEST, preferred_element_t...  28.1 us
  transfers between devices with their start and end apart: 3, of which 3 were waited for; matrix products, arithmetic and copies ran while one was open for 0% of the time, Pallas kernels for 0%

commit v1 on v0

v1 whole, which is shorter than its diff:
```python
import functools

import jax
import jax.numpy as jnp
from jax import lax
from jax.experimental import pallas as pl
from jax.experimental.pallas import tpu as pltpu
from jax.sharding import PartitionSpec as P

ITERS = 4
PAD = 64


def product(left, right):
    return jnp.dot(left, right, precision=lax.Precision.HIGHEST, preferred_element_type=jnp.float32)


def split(value):
    high = value.astype(jnp.bfloat16)
    rest = value - high.astype(jnp.float32)
    middle = rest.astype(jnp.bfloat16)
    low = (rest - middle.astype(jnp.float32)).astype(jnp.bfloat16)
    return high, middle, low


def matmul(left, right):
    return lax.dot_general(left, right, (((1,), (0,)), ((), ())), preferred_element_type=jnp.float32)


def matmul_t(left, right):
    return lax.dot_general(left, right, (((1,), (1,)), ((), ())), preferred_element_type=jnp.float32)


def inverse_factor(small, rank):
    rows = lax.broadcasted_iota(jnp.int32, (PAD, 2 * PAD), 0)
    lanes = lax.broadcasted_iota(jnp.int32, (PAD, 2 * PAD), 1)
    unit = jnp.where(lanes == rows + PAD, 1.0, 0.0)
    both = jnp.concatenate([small, jnp.zeros((PAD, PAD), jnp.float32)], axis=1) + unit
    for k in range(rank):
        row = both[k:k + 1, :]
        pivot = both[k:k + 1, k:k + 1]
        column = both[:, k:k + 1] * (1.0 / pivot)
        both = both - jnp.where(rows > k, column, 0.0) * row
    diagonal = jnp.sum(jnp.where(lanes == rows, both, 0.0), axis=1, keepdims=True)
    inside = lax.broadcasted_iota(jnp.int32, (PAD, 1), 0) < rank
    scale = jnp.where(inside, lax.rsqrt(jnp.where(inside, diagonal, 1.0)), 0.0)
    return both[:, PAD:] * scale


def subspace_kernel(rank, gram_ref, start_ref, out_ref):
    g1, g2, g3 = split(gram_ref[...])
    basis = start_ref[...]
    for _ in range(ITERS):
        b1, b2, b3 = split(basis)
        by1 = matmul(jnp.concatenate([b1, b2, b3], axis=0), g1)
        by2 = matmul(jnp.concatenate([b1, b2], axis=0), g2)
        by3 = matmul(b1, g3)
        z = (by3 + by1[2 * PAD:] + by2[PAD:]) + (by1[PAD:2 * PAD] + by2[:PAD]) + by1[:PAD]
        z1, z2, z3 = split(z)
        s = matmul_t(jnp.concatenate([z1, z2, z3], axis=0), jnp.concatenate([z1, z2, z3], axis=0))
        small = (s[:PAD, 2 * PAD:] + s[2 * PAD:, :PAD] + s[PAD:2 * PAD, PAD:2 * PAD]) + (s[:PAD, PAD:2 * PAD] + s[PAD:2 * PAD, :PAD]) + s[:PAD, :PAD]
        w1, w2, w3 = split(inverse_factor(small, rank))
        basis = (matmul(w3, z1) + matmul(w1, z3) + matmul(w2, z2)) + (matmul(w2, z1) + matmul(w1, z2)) + matmul(w1, z1)
    out_ref[...] = basis


def subspace(gram, start):
    width, rank = start.shape
    start_t = jnp.pad(start.T, ((0, PAD - rank), (0, 0)))
    return pl.pallas_call(
        functools.partial(subspace_kernel, rank),
        out_shape=jax.ShapeDtypeStruct((PAD, width), jnp.float32),
        in_specs=[pl.BlockSpec(memory_space=pltpu.VMEM)] * 2,
        out_specs=pl.BlockSpec(memory_space=pltpu.VMEM),
        compiler_params=pltpu.CompilerParams(vmem_limit_bytes=32 * 1024 * 1024),
    )(gram, start_t)


def partner(value, axis, size, bits):
    return lax.ppermute(value, axis, [(i, i ^ bits) for i in range(size)])


def spread(block, axis, size):
    return lax.all_to_all(jnp.broadcast_to(block, (size,) + block.shape), axis, 0, 0)


def per_device(field, start_x, start_y):
    rows_y, rows_z, count_var, width_x = field.shape
    rank = start_x.shape[1]
    size_y, size_z = lax.axis_size("gy"), lax.axis_size("gz")
    flat = field.reshape(rows_y * rows_z * count_var, width_x)
    columns = flat.shape[0] * size_y * size_z
    partial = product(flat.T, flat).reshape(size_y, width_x // size_y, width_x)
    block = jnp.sum(lax.all_to_all(partial, "gy", 0, 0), axis=0)
    p = [block] + [partner(block, "gz", size_z, bits) for bits in range(1, 8)]
    block = ((p[0] + p[1]) + (p[2] + p[3])) + ((p[4] + p[5]) + (p[6] + p[7]))
    p = [block] + [partner(block, "gz", size_z, bits) for bits in (8, 16, 24)]
    block = ((p[0] + p[1]) + (p[2] + p[3])) / columns
    gram_x = spread(block, "gy", size_y).reshape(width_x, width_x)
    factor_x = subspace(gram_x, start_x)[:rank].T
    reduced = product(flat, factor_x).reshape(rows_y, rows_z * count_var * rank)
    columns_y = rows_z * count_var * rank * size_z
    total_y = rows_y * size_y
    whole = spread(reduced, "gy", size_y).reshape(total_y, -1)
    block = product(reduced, whole.T)
    for bits in (1, 2, 4, 8, 16):
        block = block + partner(block, "gz", size_z, bits)
    gram_y = spread(block / columns_y, "gy", size_y).reshape(total_y, total_y)
    factor_t = subspace(gram_y, start_y)[:rank]
    core = product(factor_t, whole)
    first_row = lax.axis_index("gy") * rows_y
    factor_y = lax.dynamic_slice_in_dim(factor_t.T, first_row, rows_y, 0)
    core = core / jnp.sqrt(jnp.float32(width_x * total_y))
    return (factor_x, factor_y, core.reshape(rank, rows_z, count_var * rank))


def solution(mesh):
    placed = (P("gy", "gz", None, None), P(), P())
    return jax.shard_map(
        per_device,
        mesh=mesh,
        in_specs=placed,
        out_specs=(P(), P("gy", None), P(None, "gz", None)),
        check_vma=False,
    )
```

time: 879 us -> 261 us (0.30)
  waiting for transfers between devices: 734 us -> 54 us
  other arithmetic: 91.3 us -> 0.15 us
  starting transfers between devices: 0.52 us -> 71.2 us
  blocking collectives: 0 us -> 61.5 us
  Pallas kernels: 0 us -> 48.1 us
  matrix products: 30.5 us -> 10.1 us
  between operations: 14.1 us -> 0.93 us
    psum x2 -> x0, waiting for transfers between devices: 675 us -> none  [the longest x1 469 us: per_device(): gram_x = lax.psum(product(flat.T, flat), ('gy', 'gz')) / columns]
    another operation x40 -> x0, other arithmetic: 91.2 us -> none  [the longest x24 49.3 us: orthonormal(): lower = jnp.linalg.cholesky(small)]
    ppermute x0 -> x15, starting transfers between devices: none -> 63.6 us  [partner(): return lax.ppermute(value, axis, [(i, i ^ bits) for i in range(size)])]
    all_to_all x0 -> x2, blocking collectives: none -> 61.5 us  [the longest x1 38.7 us: spread(): lax.all_to_all(jnp.broadcast_to(block, (size,) + block.shape), axis, 0, 0)]
    all_gather x1 -> x0, waiting for transfers between devices: 58.9 us -> none  [per_device(): whole = lax.all_gather(reduced, 'gy', axis=0, tiled=True)]
    pallas_call x0 -> x2, Pallas kernels: none -> 48.1 us  [subspace(): pl.pallas_call(functools.partial(subspace_kernel, rank), out_shape=jax.Sh...]
    ppermute x0 -> x15, waiting for transfers between devices: none -> 31.1 us  [partner(): return lax.ppermute(value, axis, [(i, i ^ bits) for i in range(size)])]
    all_to_all x0 -> x2, waiting for transfers between devices: none -> 22.9 us  [spread(): lax.all_to_all(jnp.broadcast_to(block, (size,) + block.shape), axis, 0, 0)]
  transfers between devices with their start and end apart: 3 -> 17, of which waited for: 3 -> 11; matrix products, arithmetic and copies ran while one was open for 0% -> 0% of each run, Pallas kernels for 0% -> 0%
where the time goes in v1:
time: 261 us; the launch traced here: 256 us
  starting transfers between devices  71.2 us (27%)
  blocking collectives  61.5 us (24%)
  waiting for transfers between devices  54 us (21%)
  Pallas kernels  48.1 us (18%)
  local copies, waits for them, and re-layouts  10.4 us (4%)
  matrix products  10.1 us (4%)
    ppermute x15, starting transfers between devices, partner(): return lax.ppermute(value, axis, [(i, i ^ bits) for i in range(size)])  63.6 us
    pallas_call x2, Pallas kernels, subspace(): pl.pallas_call(functools.partial(subspace_kernel, rank), out_shape=jax.Sh...  48.1 us
    all_to_all x1, blocking collectives, spread(): lax.all_to_all(jnp.broadcast_to(block, (size,) + block.shape), axis, 0, 0)  38.7 us
    ppermute x15, waiting for transfers between devices, partner(): return lax.ppermute(value, axis, [(i, i ^ bits) for i in range(size)])  31.1 us
    all_to_all x2, waiting for transfers between devices, spread(): lax.all_to_all(jnp.broadcast_to(block, (size,) + block.shape), axis, 0, 0)  22.9 us
    all_to_all x1, blocking collectives, per_device(): block = jnp.sum(lax.all_to_all(partial, 'gy', 0, 0), axis=0)  22.8 us
    dot_general x4, matrix products, product(): jnp.dot(left, right, precision=lax.Precision.HIGHEST, preferred_element_t...  10.1 us
    all_to_all x2, starting transfers between devices, spread(): lax.all_to_all(jnp.broadcast_to(block, (size,) + block.shape), axis, 0, 0)  7.59 us
  transfers between devices with their start and end apart: 17, of which 11 were waited for; matrix products, arithmetic and copies ran while one was open for 0% of the time, Pallas kernels for 0%

profile of v1, /device:TPU:1, one launch (start us, length us, event | category | flops | bytes accessed | tf_op | source)
XLA Modules:
  0.0 256.4 jit_solution(11938802732051505221)
XLA Ops:
  0.6 1.9 copy.12
  2.5 0.2 reshape.26
  2.8 1.3 reshape.32
  4.1 0.5 copy.13
  4.6 4.0 %fusion.2 = f32[16,32,512]{2,1,0:T(8,128)S(1)} fusion(f32[16,32,704]{2,1,0:T(8,128)S(1)} %bitcast.26, f32[704,512,1]{1,0,2:T(8,128)} %reshape.32), kind=kOutput, calls=%fused_computation.9 | convolution fusion | flops 2214592512 | bytes 3932160 | tf_op jit(solution)/shard_map/dot_general | solution.py:15
  8.6 22.8 %all_to_all.20 = f32[16,32,512]{2,1,0:T(8,128)S(1)} all-to-all(f32[16,32,512]{2,1,0:T(8,128)S(1)} %fusion.2), channel_id=1, replica_groups=mesh['gy'=16,'gz'=32] {'gy'}, dimensions={0} | all-to-all | bytes 2097152 | tf_op jit(solution)/shard_map/all_to_all | solution.py:94
  31.4 0.1 reduce_sum.9
  31.5 8.8 %collective-permute-start.6 = (f32[32,512]{1,0:T(8,128)S(1)}, f32[32,512]{1,0:T(8,128)S(1)}, u32[]{:S(2)}, u32[]{:S(2)}) collective-permute-start(f32[32,512]{1,0:T(8,128)S(1)} %reduce_sum.9), channel_id=1, source_target_pairs={{0,7},{1,6},{2,5},{3,4},{4,3},{5,2},{6,1},{7,0},{8,15},{9,14},{10,... | collective-permute-start | bytes 196616 | tf_op jit(solution)/shard_map/ppermute | solution.py:80
  40.3 1.9 collective-permute-start.5
  42.2 1.9 collective-permute-start.4
  44.2 4.6 %collective-permute-start.3 = (f32[32,512]{1,0:T(8,128)S(1)}, f32[32,512]{1,0:T(8,128)S(1)}, u32[]{:S(2)}, u32[]{:S(2)}) collective-permute-start(f32[32,512]{1,0:T(8,128)S(1)} %reduce_sum.9), channel_id=1, source_target_pairs={{0,4},{1,5},{2,6},{3,7},{4,0},{5,1},{6,2},{7,3},{8,12},{9,13},{10,... | collective-permute-start | bytes 196616 | tf_op jit(solution)/shard_map/ppermute | solution.py:80
  48.8 3.1 %collective-permute-start.2 = (f32[32,512]{1,0:T(8,128)S(1)}, f32[32,512]{1,0:T(8,128)S(1)}, u32[]{:S(2)}, u32[]{:S(2)}) collective-permute-start(f32[32,512]{1,0:T(8,128)S(1)} %reduce_sum.9), channel_id=1, source_target_pairs={{0,3},{1,2},{2,1},{3,0},{4,7},{5,6},{6,5},{7,4},{8,11},{9,10},{10,... | collective-permute-start | bytes 196616 | tf_op jit(solution)/shard_map/ppermute | solution.py:80
  51.8 0.0 collective-permute-done.6
  51.8 2.5 collective-permute-start.1
  54.3 0.0 collective-permute-done.5
  54.3 2.4 collective-permute-start
  56.7 0.0 collective-permute-done.4
  56.7 0.0 collective-permute-done.3
  56.7 0.0 collective-permute-done.2
  56.7 0.7 collective-permute-done.1
  57.4 0.2 collective-permute-done
  57.6 11.3 %collective-permute-start.9 = (f32[32,512]{1,0:T(8,128)S(1)}, f32[32,512]{1,0:T(8,128)S(1)}, u32[]{:S(2)}, u32[]{:S(2)}) collective-permute-start(f32[32,512]{1,0:T(8,128)S(1)} %add_add_fusion), channel_id=1, source_target_pairs={{0,24},{1,25},{2,26},{3,27},{4,28},{5,29},{6,30},{7,31},{8,16},{9,... | collective-permute-start | bytes 196616 | tf_op jit(solution)/shard_map/ppermute | solution.py:80
  68.9 4.9 %collective-permute-start.8 = (f32[32,512]{1,0:T(8,128)S(1)}, f32[32,512]{1,0:T(8,128)S(1)}, u32[]{:S(2)}, u32[]{:S(2)}) collective-permute-start(f32[32,512]{1,0:T(8,128)S(1)} %add_add_fusion), channel_id=1, source_target_pairs={{0,16},{1,17},{2,18},{3,19},{4,20},{5,21},{6,22},{7,23},{8,24},{9,... | collective-permute-start | bytes 196616 | tf_op jit(solution)/shard_map/ppermute | solution.py:80
  73.8 4.0 %collective-permute-start.7 = (f32[32,512]{1,0:T(8,128)S(1)}, f32[32,512]{1,0:T(8,128)S(1)}, u32[]{:S(2)}, u32[]{:S(2)}) collective-permute-start(f32[32,512]{1,0:T(8,128)S(1)} %add_add_fusion), channel_id=1, source_target_pairs={{0,8},{1,9},{2,10},{3,11},{4,12},{5,13},{6,14},{7,15},{8,0},{9,1},... | collective-permute-start | bytes 196616 | tf_op jit(solution)/shard_map/ppermute | solution.py:80
  77.8 0.0 collective-permute-done.9
  77.8 8.8 %collective-permute-done.8 = f32[32,512]{1,0:T(8,128)S(1)} collective-permute-done((f32[32,512]{1,0:T(8,128)S(1)}, f32[32,512]{1,0:T(8,128)S(1)}, u32[]{:S(2)}, u32[]{:S(2)}) %collective-permute-start.8) | collective-permute-done | bytes 65568 | tf_op jit(solution)/shard_map/ppermute | solution.py:80
  86.6 3.7 %collective-permute-done.7 = f32[32,512]{1,0:T(8,128)S(1)} collective-permute-done((f32[32,512]{1,0:T(8,128)S(1)}, f32[32,512]{1,0:T(8,128)S(1)}, u32[]{:S(2)}, u32[]{:S(2)}) %collective-permute-start.7) | collective-permute-done | bytes 65568 | tf_op jit(solution)/shard_map/ppermute | solution.py:80
  90.3 0.0 copy-start
  90.3 1.1 broadcast_in_dim.9
  91.4 3.8 %all-to-all-start.1 = ((f32[16,32,512]{2,1,0:T(8,128)}), f32[16,32,512]{2,1,0:T(8,128)S(1)}, u32[]{:S(2)}, u32[]{:S(2)}) async-start(f32[16,32,512]{2,1,0:T(8,128)} %broadcast_in_dim.9), calls=%async_computation.1 | async-start | bytes 2097152 | tf_op jit(solution)/shard_map/all_to_all | solution.py:84
  95.3 0.0 copy-done
  95.3 16.3 %all-to-all-done.1 = f32[16,32,512]{2,1,0:T(8,128)S(1)} async-done(((f32[16,32,512]{2,1,0:T(8,128)}), f32[16,32,512]{2,1,0:T(8,128)S(1)}, u32[]{:S(2)}, u32[]{:S(2)}) %all-to-all-start.1) | async-done | bytes 1048608 | tf_op jit(solution)/shard_map/all_to_all | solution.py:84
  111.6 24.8 %shard_map.58 = f32[64,512]{1,0:T(8,128)S(1)} custom-call(f32[512,512]{1,0:T(8,128)S(1)} %bitcast.20, f32[64,512]{1,0:T(8,128)S(1)} %pad.8.start_ref), custom_call_target="tpu_custom_call" | custom-call | tf_op jit(solution)/shard_map/pallas_call | solution.py:70
  136.4 1.4 convolution_bitcast_fusion
  137.9 0.2 copy.14
  138.0 0.2 reshape.28
  138.2 0.2 broadcast_in_dim.10
  138.4 38.7 %all_to_all.21 = f32[16,16,2640]{2,1,0:T(8,128)S(1)} all-to-all(f32[16,16,2640]{2,1,0:T(8,128)S(1)} %broadcast_in_dim.10), channel_id=1, replica_groups=mesh['gy'=16,'gz'=32] {'gy'}, dimensions={0} | all-to-all | bytes 5406720 | tf_op jit(solution)/shard_map/all_to_all | solution.py:84
  177.1 0.0 copy-start.1
  177.1 2.2 fusion.3
  179.3 3.8 %collective-permute-start.10 = (f32[16,256]{1,0:T(8,128)S(1)}, f32[16,256]{1,0:T(8,128)S(1)}, u32[]{:S(2)}, u32[]{:S(2)}) collective-permute-start(f32[16,256]{1,0:T(8,128)S(1)} %fusion.3), channel_id=1, source_target_pairs={{0,1},{1,0},{2,3},{3,2},{4,5},{5,4},{6,7},{7,6},{8,9},{9,8},{10,11... | collective-permute-start | bytes 49160 | tf_op jit(solution)/shard_map/ppermute | solution.py:80
  183.1 0.8 collective-permute-done.10
  183.9 1.9 collective-permute-start.11
  185.9 2.6 collective-permute-done.11
  188.4 1.9 collective-permute-start.12
  190.3 3.5 %collective-permute-done.12 = f32[16,256]{1,0:T(8,128)S(1)} collective-permute-done((f32[16,256]{1,0:T(8,128)S(1)}, f32[16,256]{1,0:T(8,128)S(1)}, u32[]{:S(2)}, u32[]{:S(2)}) %collective-permute-start.12) | collective-permute-done | bytes 16416 | tf_op jit(solution)/shard_map/ppermute | solution.py:80
  193.8 2.3 collective-permute-start.13
  196.1 6.2 %collective-permute-done.13 = f32[16,256]{1,0:T(8,128)S(1)} collective-permute-done((f32[16,256]{1,0:T(8,128)S(1)}, f32[16,256]{1,0:T(8,128)S(1)}, u32[]{:S(2)}, u32[]{:S(2)}) %collective-permute-start.13) | collective-permute-done | bytes 16416 | tf_op jit(solution)/shard_map/ppermute | solution.py:80
  202.3 8.4 %collective-permute-start.14 = (f32[16,256]{1,0:T(8,128)S(1)}, f32[16,256]{1,0:T(8,128)S(1)}, u32[]{:S(2)}, u32[]{:S(2)}) collective-permute-start(f32[16,256]{1,0:T(8,128)S(1)} %add.65), channel_id=1, source_target_pairs={{0,16},{1,17},{2,18},{3,19},{4,20},{5,21},{6,22},{7,23},{8,24},{9,... | collective-permute-start | bytes 49160 | tf_op jit(solution)/shard_map/ppermute | solution.py:80
  210.7 4.8 %collective-permute-done.14 = f32[16,256]{1,0:T(8,128)S(1)} collective-permute-done((f32[16,256]{1,0:T(8,128)S(1)}, f32[16,256]{1,0:T(8,128)S(1)}, u32[]{:S(2)}, u32[]{:S(2)}) %collective-permute-start.14) | collective-permute-done | bytes 16416 | tf_op jit(solution)/shard_map/ppermute | solution.py:80
  215.4 0.7 broadcast_in_dim.11
  216.2 3.8 %all-to-all-start.3 = ((f32[16,16,256]{2,1,0:T(8,128)}), f32[16,16,256]{2,1,0:T(8,128)S(1)}, u32[]{:S(2)}, u32[]{:S(2)}) async-start(f32[16,16,256]{2,1,0:T(8,128)} %broadcast_in_dim.11), calls=%async_computation.3 | async-start | bytes 524288 | tf_op jit(solution)/shard_map/all_to_all | solution.py:84
  219.9 0.0 copy-done.1
  220.0 0.7 slice_bitcast_fusion
  220.6 6.6 %all-to-all-done.3 = f32[16,16,256]{2,1,0:T(8,128)S(1)} async-done(((f32[16,16,256]{2,1,0:T(8,128)}), f32[16,16,256]{2,1,0:T(8,128)S(1)}, u32[]{:S(2)}, u32[]{:S(2)}) %all-to-all-start.3) | async-done | bytes 262176 | tf_op jit(solution)/shard_map/all_to_all | solution.py:84
  227.2 23.3 %shard_map.59 = f32[64,256]{1,0:T(8,128)S(1)} custom-call(f32[256,256]{1,0:T(8,128)S(1)} %bitcast.21, f32[64,256]{1,0:T(8,128)S(1)} %pad.9.start_ref), custom_call_target="tpu_custom_call" | custom-call | tf_op jit(solution)/shard_map/pallas_call | solution.py:70
  250.6 2.4 convolution_multiply_fusion
  253.0 0.1 dynamic-slice_bitcast_fusion
  253.1 0.7 copy.15
  253.8 2.6 %reshape.31 = f32[60,4,660]{2,1,0:T(4,128)} reshape(f32[60,2640]{1,0:T(8,128)} %convolution_multiply_fusion) | data formatting | bytes 1267200 | tf_op jit(solution)/shard_map/reshape | solution.py:114
  (9 shorter events, 0.1 us)
Async XLA Ops:
  31.5 20.3 %collective-permute-start.6 = (f32[32,512]{1,0:T(8,128)S(1)}, f32[32,512]{1,0:T(8,128)S(1)}, u32[]{:S(2)}, u32[]{:S(2)}) collective-permute-start(f32[32,512]{1,0:T(8,128)S(1)} %reduce_sum.9), channel_id=1, source_target_pairs={{0,7},{1,6},{2,5},{3,4},{4,3},{5,2},{6,1},{7,0},{8,15},{9,14},{10,... | collective-permute-start | bytes 196616 | tf_op jit(solution)/shard_map/ppermute | solution.py:80
  40.3 14.0 %collective-permute-start.5 = (f32[32,512]{1,0:T(8,128)S(1)}, f32[32,512]{1,0:T(8,128)S(1)}, u32[]{:S(2)}, u32[]{:S(2)}) collective-permute-start(f32[32,512]{1,0:T(8,128)S(1)} %reduce_sum.9), channel_id=1, source_target_pairs={{0,6},{1,7},{2,4},{3,5},{4,2},{5,3},{6,0},{7,1},{8,14},{9,15},{10,... | collective-permute-start | bytes 196616 | tf_op jit(solution)/shard_map/ppermute | solution.py:80
  42.2 14.4 %collective-permute-start.4 = (f32[32,512]{1,0:T(8,128)S(1)}, f32[32,512]{1,0:T(8,128)S(1)}, u32[]{:S(2)}, u32[]{:S(2)}) collective-permute-start(f32[32,512]{1,0:T(8,128)S(1)} %reduce_sum.9), channel_id=1, source_target_pairs={{0,5},{1,4},{2,7},{3,6},{4,1},{5,0},{6,3},{7,2},{8,13},{9,12},{10,... | collective-permute-start | bytes 196616 | tf_op jit(solution)/shard_map/ppermute | solution.py:80
  44.2 12.5 %collective-permute-start.3 = (f32[32,512]{1,0:T(8,128)S(1)}, f32[32,512]{1,0:T(8,128)S(1)}, u32[]{:S(2)}, u32[]{:S(2)}) collective-permute-start(f32[32,512]{1,0:T(8,128)S(1)} %reduce_sum.9), channel_id=1, source_target_pairs={{0,4},{1,5},{2,6},{3,7},{4,0},{5,1},{6,2},{7,3},{8,12},{9,13},{10,... | collective-permute-start | bytes 196616 | tf_op jit(solution)/shard_map/ppermute | solution.py:80
  48.8 7.9 %collective-permute-start.2 = (f32[32,512]{1,0:T(8,128)S(1)}, f32[32,512]{1,0:T(8,128)S(1)}, u32[]{:S(2)}, u32[]{:S(2)}) collective-permute-start(f32[32,512]{1,0:T(8,128)S(1)} %reduce_sum.9), channel_id=1, source_target_pairs={{0,3},{1,2},{2,1},{3,0},{4,7},{5,6},{6,5},{7,4},{8,11},{9,10},{10,... | collective-permute-start | bytes 196616 | tf_op jit(solution)/shard_map/ppermute | solution.py:80
  51.8 5.6 %collective-permute-start.1 = (f32[32,512]{1,0:T(8,128)S(1)}, f32[32,512]{1,0:T(8,128)S(1)}, u32[]{:S(2)}, u32[]{:S(2)}) collective-permute-start(f32[32,512]{1,0:T(8,128)S(1)} %reduce_sum.9), channel_id=1, source_target_pairs={{0,2},{1,3},{2,0},{3,1},{4,6},{5,7},{6,4},{7,5},{8,10},{9,11},{10,... | collective-permute-start | bytes 196616 | tf_op jit(solution)/shard_map/ppermute | solution.py:80
  54.3 3.2 %collective-permute-start = (f32[32,512]{1,0:T(8,128)S(1)}, f32[32,512]{1,0:T(8,128)S(1)}, u32[]{:S(2)}, u32[]{:S(2)}) collective-permute-start(f32[32,512]{1,0:T(8,128)S(1)} %reduce_sum.9), channel_id=1, source_target_pairs={{0,1},{1,0},{2,3},{3,2},{4,5},{5,4},{6,7},{7,6},{8,9},{9,8},{10,11... | collective-permute-start | bytes 196616 | tf_op jit(solution)/shard_map/ppermute | solution.py:80
  57.6 20.2 %collective-permute-start.9 = (f32[32,512]{1,0:T(8,128)S(1)}, f32[32,512]{1,0:T(8,128)S(1)}, u32[]{:S(2)}, u32[]{:S(2)}) collective-permute-start(f32[32,512]{1,0:T(8,128)S(1)} %add_add_fusion), channel_id=1, source_target_pairs={{0,24},{1,25},{2,26},{3,27},{4,28},{5,29},{6,30},{7,31},{8,16},{9,... | collective-permute-start | bytes 196616 | tf_op jit(solution)/shard_map/ppermute | solution.py:80
  68.9 17.7 %collective-permute-start.8 = (f32[32,512]{1,0:T(8,128)S(1)}, f32[32,512]{1,0:T(8,128)S(1)}, u32[]{:S(2)}, u32[]{:S(2)}) collective-permute-start(f32[32,512]{1,0:T(8,128)S(1)} %add_add_fusion), channel_id=1, source_target_pairs={{0,16},{1,17},{2,18},{3,19},{4,20},{5,21},{6,22},{7,23},{8,24},{9,... | collective-permute-start | bytes 196616 | tf_op jit(solution)/shard_map/ppermute | solution.py:80
  73.8 16.5 %collective-permute-start.7 = (f32[32,512]{1,0:T(8,128)S(1)}, f32[32,512]{1,0:T(8,128)S(1)}, u32[]{:S(2)}, u32[]{:S(2)}) collective-permute-start(f32[32,512]{1,0:T(8,128)S(1)} %add_add_fusion), channel_id=1, source_target_pairs={{0,8},{1,9},{2,10},{3,11},{4,12},{5,13},{6,14},{7,15},{8,0},{9,1},... | collective-permute-start | bytes 196616 | tf_op jit(solution)/shard_map/ppermute | solution.py:80
  90.3 5.0 %copy-start = (f32[512,60]{0,1:T(8,128)S(1)}, f32[512,60]{0,1:T(8,128)}, u32[]{:S(2)}) copy-start(f32[512,60]{0,1:T(8,128)} %param.4) | copy-start | bytes 368644
  91.4 20.2 %all-to-all-start.1 = ((f32[16,32,512]{2,1,0:T(8,128)}), f32[16,32,512]{2,1,0:T(8,128)S(1)}, u32[]{:S(2)}, u32[]{:S(2)}) async-start(f32[16,32,512]{2,1,0:T(8,128)} %broadcast_in_dim.9), calls=%async_computation.1 | async-start | bytes 2097152 | tf_op jit(solution)/shard_map/all_to_all | solution.py:84
  177.1 42.9 %copy-start.1 = (f32[256,60]{0,1:T(8,128)S(1)}, f32[256,60]{0,1:T(8,128)}, u32[]{:S(2)}) copy-start(f32[256,60]{0,1:T(8,128)} %param.5) | copy-start | bytes 184324
  179.3 4.6 %collective-permute-start.10 = (f32[16,256]{1,0:T(8,128)S(1)}, f32[16,256]{1,0:T(8,128)S(1)}, u32[]{:S(2)}, u32[]{:S(2)}) collective-permute-start(f32[16,256]{1,0:T(8,128)S(1)} %fusion.3), channel_id=1, source_target_pairs={{0,1},{1,0},{2,3},{3,2},{4,5},{5,4},{6,7},{7,6},{8,9},{9,8},{10,11... | collective-permute-start | bytes 49160 | tf_op jit(solution)/shard_map/ppermute | solution.py:80
  183.9 4.5 %collective-permute-start.11 = (f32[16,256]{1,0:T(8,128)S(1)}, f32[16,256]{1,0:T(8,128)S(1)}, u32[]{:S(2)}, u32[]{:S(2)}) collective-permute-start(f32[16,256]{1,0:T(8,128)S(1)} %add.62), channel_id=1, source_target_pairs={{0,2},{1,3},{2,0},{3,1},{4,6},{5,7},{6,4},{7,5},{8,10},{9,11},{10,... | collective-permute-start | bytes 49160 | tf_op jit(solution)/shard_map/ppermute | solution.py:80
  188.4 5.4 %collective-permute-start.12 = (f32[16,256]{1,0:T(8,128)S(1)}, f32[16,256]{1,0:T(8,128)S(1)}, u32[]{:S(2)}, u32[]{:S(2)}) collective-permute-start(f32[16,256]{1,0:T(8,128)S(1)} %add.63), channel_id=1, source_target_pairs={{0,4},{1,5},{2,6},{3,7},{4,0},{5,1},{6,2},{7,3},{8,12},{9,13},{10,... | collective-permute-start | bytes 49160 | tf_op jit(solution)/shard_map/ppermute | solution.py:80
  193.8 8.5 %collective-permute-start.13 = (f32[16,256]{1,0:T(8,128)S(1)}, f32[16,256]{1,0:T(8,128)S(1)}, u32[]{:S(2)}, u32[]{:S(2)}) collective-permute-start(f32[16,256]{1,0:T(8,128)S(1)} %add.64), channel_id=1, source_target_pairs={{0,8},{1,9},{2,10},{3,11},{4,12},{5,13},{6,14},{7,15},{8,0},{9,1},... | collective-permute-start | bytes 49160 | tf_op jit(solution)/shard_map/ppermute | solution.py:80
  202.3 13.2 %collective-permute-start.14 = (f32[16,256]{1,0:T(8,128)S(1)}, f32[16,256]{1,0:T(8,128)S(1)}, u32[]{:S(2)}, u32[]{:S(2)}) collective-permute-start(f32[16,256]{1,0:T(8,128)S(1)} %add.65), channel_id=1, source_target_pairs={{0,16},{1,17},{2,18},{3,19},{4,20},{5,21},{6,22},{7,23},{8,24},{9,... | collective-permute-start | bytes 49160 | tf_op jit(solution)/shard_map/ppermute | solution.py:80
  216.2 11.0 %all-to-all-start.3 = ((f32[16,16,256]{2,1,0:T(8,128)}), f32[16,16,256]{2,1,0:T(8,128)S(1)}, u32[]{:S(2)}, u32[]{:S(2)}) async-start(f32[16,16,256]{2,1,0:T(8,128)} %broadcast_in_dim.11), calls=%async_computation.3 | async-start | bytes 524288 | tf_op jit(solution)/shard_map/all_to_all | solution.py:84

commit v2 on v0

v2 whole, which is shorter than its diff:
```python
import functools

import jax
import jax.numpy as jnp
from jax import lax
from jax.experimental import pallas as pl
from jax.experimental.pallas import tpu as pltpu
from jax.sharding import PartitionSpec as P

ITERS = 4
PAD = 64
LANES = 128
PANEL = 4
PLANE = ("gy", "core")
VMEM = pl.BlockSpec(memory_space=pltpu.VMEM)
LIMIT = pltpu.CompilerParams(vmem_limit_bytes=48 * 1024 * 1024)


def split2(value):
    high = value.astype(jnp.bfloat16)
    return high, (value - high.astype(jnp.float32)).astype(jnp.bfloat16)


def split3(value):
    high = value.astype(jnp.bfloat16)
    rest = value - high.astype(jnp.float32)
    middle = rest.astype(jnp.bfloat16)
    return high, middle, (rest - middle.astype(jnp.float32)).astype(jnp.bfloat16)


def dot(left, right, dims):
    return lax.dot_general(left, right, ((dims[:1], dims[1:]), ((), ())), preferred_element_type=jnp.float32)


def upper_blocks(count):
    return [(i, j) for i in range(count) for j in range(i, count)]


def unpack(packed_ref, width):
    count = width // LANES
    blocks = {
        pair: packed_ref[LANES * n:LANES * (n + 1), :] for n, pair in enumerate(upper_blocks(count))
    }
    rows = [
        jnp.concatenate([blocks[(i, j)] if i <= j else blocks[(j, i)].T for j in range(count)], axis=1)
        for i in range(count)
    ]
    return jnp.concatenate(rows, axis=0)


def unit_trace(gram):
    eye = lax.broadcasted_iota(jnp.int32, gram.shape, 0) == lax.broadcasted_iota(jnp.int32, gram.shape, 1)
    diagonal = jnp.sum(jnp.where(eye, gram, 0.0), axis=0, keepdims=True)
    return gram * (1.0 / jnp.sum(diagonal, axis=1, keepdims=True))


def inverse_factor(small, rank):
    iota = functools.partial(lax.broadcasted_iota, jnp.int32)
    rows, lanes = iota((PAD, 2 * PAD), 0), iota((PAD, 2 * PAD), 1)
    both = jnp.concatenate([small, jnp.zeros((PAD, PAD), jnp.float32)], axis=1)
    both = both + jnp.where(lanes == rows + PAD, 1.0, 0.0)
    tiles = [both[8 * t:8 * t + 8, :] for t in range(PAD // 8)]
    within = iota((8, LANES), 0)
    for start in range(0, rank, PANEL):
        first = start // 8
        cols = [
            {t: jnp.broadcast_to(tiles[t][:, start + j:start + j + 1], (8, LANES)) for t in range(first, PAD // 8)}
            for j in range(PANEL)
        ]
        base = start - 8 * first
        lines = [jnp.broadcast_to(tiles[first][base + j:base + j + 1, :], (8, LANES)) for j in range(PANEL)]
        factors = []
        for j in range(PANEL):
            def at(column, row):
                return jnp.broadcast_to(column[first][base + row:base + row + 1, :], (8, LANES))
            inverse = 1.0 / at(cols[j], j)
            factor = {t: column * inverse for t, column in cols[j].items()}
            ahead = [at(cols[n], j) for n in range(j + 1, PANEL)]
            factor[first] = jnp.where(within > base + j, factor[first], 0.0)
            for n in range(j + 1, PANEL):
                lines[n] = lines[n] - at(factor, n) * lines[j]
                cols[n] = {t: column - factor[t] * ahead[n - j - 1] for t, column in cols[n].items()}
            factors.append(factor)
        for t in range(first, PAD // 8):
            change = factors[0][t] * lines[0]
            for j in range(1, PANEL):
                change = change + factors[j][t] * lines[j]
            tiles[t] = tiles[t] - change
    both = jnp.concatenate(tiles, axis=0)
    diagonal = jnp.sum(jnp.where(lanes == rows, both, 0.0), axis=1, keepdims=True)
    inside = iota((PAD, 1), 0) < rank
    scale = jnp.where(inside, lax.rsqrt(jnp.where(inside, diagonal, 1.0)), 0.0)
    return both[:, PAD:] * scale


def subspace(gram, basis, rank):
    g1, g2, g3 = split3(gram)
    for step in range(ITERS):
        b1, b2, b3 = split3(basis)
        by1 = dot(jnp.concatenate([b1, b2, b3], axis=0), g1, (1, 0))
        by2 = dot(jnp.concatenate([b1, b2], axis=0), g2, (1, 0))
        by3 = dot(b1, g3, (1, 0))
        z = (by3 + by1[2 * PAD:] + by2[PAD:]) + (by1[PAD:2 * PAD] + by2[:PAD]) + by1[:PAD]
        basis = z
        if step % 2 == 0:
            continue
        z1, z2, z3 = split3(z)
        zs = jnp.concatenate([z1, z2, z3], axis=0)
        s = dot(zs, zs, (1, 1))
        small = (s[:PAD, 2 * PAD:] + s[2 * PAD:, :PAD] + s[PAD:2 * PAD, PAD:2 * PAD]) + (s[:PAD, PAD:2 * PAD] + s[PAD:2 * PAD, :PAD]) + s[:PAD, :PAD]
        w1, w2, w3 = split3(inverse_factor(small, rank))
        left = jnp.concatenate([w1, w1, w2, w2, w1, w3], axis=1)
        right = jnp.concatenate([z1, z2, z1, z2, z3, z1], axis=0)
        basis = dot(left, right, (1, 0))
    return basis


def padded(start_ref):
    rank, width = start_ref.shape
    return jnp.concatenate([start_ref[...], jnp.zeros((PAD - rank, width), jnp.float32)], axis=0)


def gram_kernel(dims, field_ref, packed_ref, high_ref, middle_ref):
    count_y, count_v, count_z, tiles_x = dims
    stride = count_v * tiles_x * count_z
    rows = []
    for z in range(count_z):
        for v in range(count_v):
            rows.append(jnp.concatenate(
                [field_ref[pl.ds((v * tiles_x + t) * count_z + z, count_y, stride=stride), :] for t in range(tiles_x)], axis=1))
    high, middle = split2(jnp.concatenate(rows, axis=0))
    high_ref[...] = high
    middle_ref[...] = middle
    done = 0
    for i in range(tiles_x // 2):
        part = slice(2 * LANES * i, 2 * LANES * (i + 1))
        rest = slice(2 * LANES * i, None)
        gram = dot(high[:, part], middle[:, rest], (0, 0)) + dot(middle[:, part], high[:, rest], (0, 0))
        gram = gram + dot(high[:, part], high[:, rest], (0, 0))
        for half in range(2):
            for j in range(half, gram.shape[1] // LANES):
                packed_ref[done:done + LANES, :] = gram[LANES * half:LANES * (half + 1), LANES * j:LANES * (j + 1)]
                done += LANES


def x_kernel(packed_ref, start_ref, high_ref, middle_ref, factor_ref, chunks_ref, pairs_ref):
    rank, width = start_ref.shape
    devices, count_y, _ = chunks_ref.shape
    basis = subspace(unit_trace(unpack(packed_ref, width)), padded(start_ref), rank)
    factor_ref[...] = basis[:rank]
    f1, f2 = split2(basis)
    high, middle = high_ref[...], middle_ref[...]
    reduced = (dot(high, f2, (1, 1)) + dot(middle, f1, (1, 1))) + dot(high, f1, (1, 1))
    count = reduced.shape[0] // count_y
    blocks = [reduced[count_y * n:count_y * (n + 1), :] for n in range(count)]
    blank = jnp.zeros((count_y, PAD), jnp.float32)
    per = chunks_ref.shape[2] // PAD
    for d in range(devices):
        parts = [blocks[n] if n < count else blank for n in range(per * d, per * (d + 1))]
        chunks_ref[d] = jnp.concatenate(parts, axis=1)
    for n in range(count // 2):
        pairs_ref[count_y * n:count_y * (n + 1), :] = jnp.concatenate(blocks[2 * n:2 * n + 2], axis=1)


def y_gram_kernel(columns_ref, gram_ref):
    a1, a2 = split2(columns_ref[...])
    gram = (dot(a1, a2, (1, 1)) + dot(a2, a1, (1, 1))) + dot(a1, a1, (1, 1))
    width = gram.shape[0]
    for n in range(width // LANES):
        gram_ref[width * n:width * (n + 1), :] = gram[:, LANES * n:LANES * (n + 1)]


def y_kernel(gram_ref, start_ref, factor_ref):
    rank, width = start_ref.shape
    gram = jnp.concatenate([gram_ref[width * n:width * (n + 1), :] for n in range(width // LANES)], axis=1)
    factor_ref[...] = subspace(unit_trace(gram), padded(start_ref), rank)


def core_kernel(dims, scale, factor_ref, whole_ref, out_ref):
    rank, count_z, count_v, count_y = dims
    devices = whole_ref.shape[0]
    f1, f2 = split2(factor_ref[...])
    columns = [
        jnp.concatenate([whole_ref[d, count_y * n:count_y * (n + 1), :] for d in range(devices)], axis=0)
        for n in range(count_z * count_v // 2)
    ]
    a1, a2 = split2(jnp.concatenate(columns, axis=1))
    core = ((dot(f1, a2, (1, 0)) + dot(f2, a1, (1, 0))) + dot(f1, a1, (1, 0))) * scale
    for z in range(count_z):
        out_ref[z] = jnp.concatenate(
            [core[:rank, PAD * n:PAD * n + rank] for n in range(z * count_v, (z + 1) * count_v)], axis=1)


def call(kernel, shapes, *args):
    return pl.pallas_call(
        kernel,
        out_shape=shapes,
        in_specs=[VMEM] * len(args),
        out_specs=jax.tree.map(lambda _: VMEM, shapes),
        compiler_params=LIMIT,
    )(*args)


def shape(dims, kind=jnp.float32):
    return jax.ShapeDtypeStruct(dims, kind)


def spread(block, axes):
    copies = jnp.broadcast_to(block, (lax.axis_size(axes),) + block.shape)
    return lax.all_to_all(copies, axes, 0, 0)


def total(packed, factor):
    size = lax.axis_size(PLANE)
    parts = packed.reshape(size, packed.shape[0] // size, LANES)
    block = jnp.sum(lax.all_to_all(parts, PLANE, 0, 0), axis=0)
    block = jnp.sum(spread(block, "z"), axis=0) * factor
    return spread(block, PLANE).reshape(packed.shape)


def per_device(field, start_x, start_y):
    rows_y, rows_z, count_var, width_x = field.shape
    rank = start_x.shape[1]
    size_y, size_z = lax.axis_size("gy"), lax.axis_size(("z", "core"))
    total_y = rows_y * size_y
    tiles_x = width_x // LANES
    count = rows_z * count_var
    view = field.transpose(0, 2, 1, 3).reshape(rows_y * count_var, rows_z, tiles_x, LANES)
    view = view.transpose(0, 2, 1, 3).reshape(-1, LANES)
    blocks_x = len(upper_blocks(tiles_x))
    flat = (rows_y * count, width_x)
    packed, high, middle = call(
        functools.partial(gram_kernel, (rows_y, count_var, rows_z, tiles_x)),
        (shape((blocks_x * LANES, LANES)), shape(flat, jnp.bfloat16), shape(flat, jnp.bfloat16)),
        view)
    packed = total(packed, 1.0 / (flat[0] * size_y * size_z))
    per = -(-count // size_y)
    factor_x, chunks, pairs = call(
        x_kernel,
        (shape((rank, width_x)), shape((size_y, rows_y, per * PAD)), shape((flat[0] // 2, 2 * PAD))),
        packed, start_x.T, high, middle)
    whole = lax.all_gather(pairs, "gy")
    columns = lax.all_to_all(chunks, "gy", 0, 0).reshape(total_y, per * PAD)
    gram_y = call(y_gram_kernel, shape((total_y * (total_y // LANES), LANES)), columns)
    gram_y = total(gram_y, 1.0 / (count * rank * size_z))
    factor_t = call(y_kernel, shape((PAD, total_y)), gram_y, start_y.T)
    mine = lax.dynamic_slice_in_dim(factor_t, lax.axis_index("gy") * rows_y, rows_y, 1)
    core = call(
        functools.partial(core_kernel, (rank, rows_z, count_var, rows_y), 1.0 / float(width_x * total_y) ** 0.5),
        shape((rows_z, rank, count_var * rank)),
        factor_t, whole)
    return (factor_x.T, mine[:rank].T, core.transpose(1, 0, 2))


def solution(mesh):
    size_y, size_z = mesh.devices.shape
    inner = jax.sharding.Mesh(mesh.devices.reshape(size_y, size_z // 2, 2), ("gy", "z", "core"))
    along_z = ("z", "core")
    return jax.shard_map(
        per_device,
        mesh=inner,
        in_specs=(P("gy", along_z, None, None), P(), P()),
        out_specs=(P(), P("gy", None), P(None, along_z, None)),
        check_vma=False,
    )
```

time: 879 us -> 175 us (0.20)
  waiting for transfers between devices: 734 us -> 9.02 us
  blocking collectives: 0 us -> 118 us
  other arithmetic: 91.3 us -> 0.14 us
  matrix products: 30.5 us -> 0 us
  Pallas kernels: 0 us -> 20 us
    psum x2 -> x0, waiting for transfers between devices: 675 us -> none  [the longest x1 469 us: per_device(): gram_x = lax.psum(product(flat.T, flat), ('gy', 'gz')) / columns]
    all_to_all x0 -> x6, blocking collectives: none -> 118 us  [the longest x3 70 us: spread(): return lax.all_to_all(copies, axes, 0, 0)]
    another operation x40 -> x0, other arithmetic: 91.2 us -> none  [the longest x24 49.3 us: orthonormal(): lower = jnp.linalg.cholesky(small)]
    all_gather x1, waiting for transfers between devices: 58.9 us -> 0.01 us  [per_device(): whole = lax.all_gather(pairs, 'gy')]
    dot_general x20 -> x0, matrix products: 28.1 us -> none  [product(): jnp.dot(left, right, precision=lax.Precision.HIGHEST, preferred_element_t...]
    pallas_call x0 -> x5, Pallas kernels: none -> 20 us  [call(): pl.pallas_call(kernel, out_shape=shapes, in_specs=[VMEM] * len(args), out...]
    all_to_all x0 -> x1, waiting for transfers between devices: none -> 9 us  [spread(): return lax.all_to_all(copies, axes, 0, 0)]
  transfers between devices with their start and end apart: 3 -> 2, of which waited for: 3 -> 1; matrix products, arithmetic and copies ran while one was open for 0% -> 1% of each run, Pallas kernels for 0% -> 4%
where the time goes in v2:
time: 175 us; the launch traced here: 174 us
  blocking collectives  118 us (67%)
  Pallas kernels  20 us (11%)
  between operations  14.1 us (8%)
  waiting for transfers between devices  9.02 us (5%)
  starting transfers between devices  7.21 us (4%)
  local copies, waits for them, and re-layouts  6.08 us (3%)
    all_to_all x3, blocking collectives, spread(): return lax.all_to_all(copies, axes, 0, 0)  70 us
    all_to_all x2, blocking collectives, total(): block = jnp.sum(lax.all_to_all(parts, PLANE, 0, 0), axis=0)  35.9 us
    pallas_call x5, Pallas kernels, call(): pl.pallas_call(kernel, out_shape=shapes, in_specs=[VMEM] * len(args), out...  20 us
    all_to_all x1, blocking collectives, per_device(): columns = lax.all_to_all(chunks, 'gy', 0, 0).reshape(total_y, per * PAD)  11.6 us
    all_to_all x1, waiting for transfers between devices, spread(): return lax.all_to_all(copies, axes, 0, 0)  9 us
    all_to_all x1, starting transfers between devices, spread(): return lax.all_to_all(copies, axes, 0, 0)  7.18 us
    unnamed x10, local copies, waits for them, and re-layouts  5.2 us
  transfers between devices with their start and end apart: 2, of which 1 were waited for; matrix products, arithmetic and copies ran while one was open for 1% of the time, Pallas kernels for 4%

profile of v2, /device:TPU:1, one launch (start us, length us, event | category | flops | bytes accessed | tf_op | source)
XLA Modules:
  0.0 174.1 jit_solution(4177462715729543150)
XLA Ops:
  7.2 0.0 all-gather.3.cloned.1.call-start
  7.2 0.0 copy-start.1
  7.2 1.4 copy-done.1
  8.6 1.4 shard_map.58
  9.9 0.0 copy-start.2
  10.0 22.7 %all_to_all.35 = f32[32,40,128]{2,1,0:T(8,128)S(1)} all-to-all(f32[32,40,128]{2,1,0:T(8,128)S(1)} %bitcast.26), channel_id=1, replica_groups=mesh['gy'=16,'z'=16,'core'=2] {'gy','core'}, dimensions={0} | all-to-all | bytes 1310720 | tf_op jit(solution)/shard_map/all_to_all | solution.py:216
  32.6 0.1 reduce_sum.36
  32.7 28.6 %all_to_all.36 = f32[16,40,128]{2,1,0:T(8,128)S(1)} all-to-all(f32[16,40,128]{2,1,0:T(8,128)S(1)} %broadcast_in_dim.12), channel_id=1, replica_groups=mesh['gy'=16,'z'=16,'core'=2] {'z'}, dimensions={0} | all-to-all | bytes 655360 | tf_op jit(solution)/shard_map/all_to_all | solution.py:210
  61.5 23.2 %all_to_all.37 = f32[32,40,128]{2,1,0:T(8,128)S(1)} all-to-all(f32[32,40,128]{2,1,0:T(8,128)S(1)} %broadcast_in_dim.13), channel_id=1, replica_groups=mesh['gy'=16,'z'=16,'core'=2] {'gy','core'}, dimensions={0} | all-to-all | bytes 1310720 | tf_op jit(solution)/shard_map/all_to_all | solution.py:210
  84.7 0.0 copy-start.3
  84.7 0.0 copy-done.2
  84.7 9.7 %shard_map.59 = (f32[60,512]{1,0:T(8,128)}, f32[16,16,192]{2,1,0:T(8,128)S(1)}, f32[352,128]{1,0:T(8,128)}) custom-call(f32[1280,128]{1,0:T(8,128)S(1)} %bitcast.21, f32[60,512]{1,0:T(8,128)S(1)} %bitcast.27, bf16[704,512]{1,0:T(8,128)(2,1)S(1)} %get-tuple-element.10.high_ref, bf16[704,512]{1,0:T(8,128)(2,1)S(1)} %get-tuple-element.11.middle_ref), custom_call_target="tpu_custom_call" | custom-call | tf_op jit(solution)/shard_map/pallas_call | solution.py:195
  94.4 0.0 all-gather.3.cloned.1.call-update
  94.4 11.6 %all_to_all.38 = f32[16,16,192]{2,1,0:T(8,128)S(1)} all-to-all(f32[16,16,192]{2,1,0:T(8,128)S(1)} %get-tuple-element.13), channel_id=1, replica_groups=mesh['gy'=16,'z'=16,'core'=2] {'gy'}, dimensions={0} | all-to-all | bytes 393216 | tf_op jit(solution)/shard_map/all_to_all | solution.py:243
  106.0 0.3 shard_map.60
  106.3 13.3 %all_to_all.39 = f32[32,16,128]{2,1,0:T(8,128)S(1)} all-to-all(f32[32,16,128]{2,1,0:T(8,128)S(1)} %bitcast.25), channel_id=1, replica_groups=mesh['gy'=16,'z'=16,'core'=2] {'gy','core'}, dimensions={0} | all-to-all | bytes 524288 | tf_op jit(solution)/shard_map/all_to_all | solution.py:216
  119.6 18.2 %all_to_all.40 = f32[16,16,128]{2,1,0:T(8,128)S(1)} all-to-all(f32[16,16,128]{2,1,0:T(8,128)S(1)} %broadcast_in_dim.14), channel_id=1, replica_groups=mesh['gy'=16,'z'=16,'core'=2] {'z'}, dimensions={0} | all-to-all | bytes 262144 | tf_op jit(solution)/shard_map/all_to_all | solution.py:210
  137.8 0.7 broadcast_in_dim.15
  138.5 7.2 %all-to-all-start.6 = ((f32[32,16,128]{2,1,0:T(8,128)}), f32[32,16,128]{2,1,0:T(8,128)S(1)}, u32[]{:S(2)}, u32[]{:S(2)}) async-start(f32[32,16,128]{2,1,0:T(8,128)} %broadcast_in_dim.15), calls=%async_computation.6 | async-start | bytes 524288 | tf_op jit(solution)/shard_map/all_to_all | solution.py:210
  145.7 9.0 %all-to-all-done.6 = f32[32,16,128]{2,1,0:T(8,128)S(1)} async-done(((f32[32,16,128]{2,1,0:T(8,128)}), f32[32,16,128]{2,1,0:T(8,128)S(1)}, u32[]{:S(2)}, u32[]{:S(2)}) %all-to-all-start.6) | async-done | bytes 262176 | tf_op jit(solution)/shard_map/all_to_all | solution.py:210
  154.7 0.0 copy-done.3
  154.7 7.4 %shard_map.61.factor_ref = f32[64,256]{1,0:T(8,128)S(1)} custom-call(f32[512,128]{1,0:T(8,128)S(1)} %bitcast.23, f32[60,256]{1,0:T(8,128)S(1)} %bitcast.28), custom_call_target="tpu_custom_call" | custom-call | tf_op jit(solution)/shard_map/pallas_call | solution.py:195
  162.1 0.1 dynamic-slice_bitcast_fusion
  162.2 0.7 copy.10
  162.9 0.0 all-gather.3.cloned.1.call-done
  162.9 0.0 copy-start
  162.9 1.8 %copy-done = f32[5632,128]{1,0:T(8,128)S(1)} copy-done((f32[5632,128]{1,0:T(8,128)S(1)}, f32[5632,128]{1,0:T(8,128)}, u32[]{:S(2)}) %copy-start) | copy-done | bytes 2883608
  164.7 1.2 shard_map.62
  166.0 1.3 copy.11
  (8 shorter events, 0.2 us)
Async XLA Ops:
  7.2 155.7 %all-gather.3.cloned.1.call-start = ((), (), s32[]{:S(2)}) async-start(), calls=%async_computation.7 | async-start | bytes 3063808 | tf_op jit(solution)/shard_map/all_gather | solution.py:242
  7.2 1.4 copy-start.1
  9.9 74.7 %copy-start.2 = (f32[512,60]{0,1:T(8,128)S(1)}, f32[512,60]{0,1:T(8,128)}, u32[]{:S(2)}) copy-start(f32[512,60]{0,1:T(8,128)} %param.4) | copy-start | bytes 368644
  84.7 70.0 %copy-start.3 = (f32[256,60]{0,1:T(8,128)S(1)}, f32[256,60]{0,1:T(8,128)}, u32[]{:S(2)}) copy-start(f32[256,60]{0,1:T(8,128)} %param.5) | copy-start | bytes 184324
  138.5 16.2 %all-to-all-start.6 = ((f32[32,16,128]{2,1,0:T(8,128)}), f32[32,16,128]{2,1,0:T(8,128)S(1)}, u32[]{:S(2)}, u32[]{:S(2)}) async-start(f32[32,16,128]{2,1,0:T(8,128)} %broadcast_in_dim.15), calls=%async_computation.6 | async-start | bytes 524288 | tf_op jit(solution)/shard_map/all_to_all | solution.py:210
  162.9 1.8 %copy-start = (f32[5632,128]{1,0:T(8,128)S(1)}, f32[5632,128]{1,0:T(8,128)}, u32[]{:S(2)}) copy-start(f32[5632,128]{1,0:T(8,128)} %all-gather.3.cloned.1.call-done) | copy-start | bytes 8650756
Sparse Core Ops, SparseCore 0:
  94.5 55.3 all-gather.2
